TPU v7x, 32 devices: a whole 2x2x4 slice. The times are simulated.
32 devices in a mesh: groups: 2 (over x), block: 16 (over z, y, core).
Axes of the slice: x: 2, y: 2, z: 4, core: 2. Of those that a mesh axis runs over, the one named last changes fastest.
Arguments:
- inflow: bfloat16 [4, 256, 16, 256], P(None, ('groups', 'block')), parts along dimension 1, may hold values from -6 to 6
- speed_bin: int32 [2], P('groups'), parts along dimension 0, may hold values from 0 to 15
- bin_table: bfloat16 [16, 32], replicated, may hold values from -3 to 3
- w_in: bfloat16 [3, 3, 3, 32, 4], replicated, may hold values from -0.625 to 0.625
- w_mid: bfloat16 [3, 3, 3, 64, 32], replicated, may hold values from -0.3125 to 0.3125
- w_dec: bfloat16 [3, 3, 3, 32, 96], replicated, may hold values from -0.15625 to 0.15625
- w_out: bfloat16 [4, 32], replicated, may hold values from -1.5 to 1.5
- grad_pred: bfloat16 [4, 256, 16, 256], P(None, ('groups', 'block')), parts along dimension 1, may hold values from -0.0059814453 to 0.0059814453
Outputs:
- pred: float32 [4, 256, 16, 256], P(None, ('groups', 'block')), parts along dimension 1
- grad_w_out: float32 [8, 32], P('groups'), parts along dimension 0
- grad_w_dec: float32 [6, 3, 3, 32, 96], P('groups'), parts along dimension 0
- grad_w_mid: float32 [6, 3, 3, 64, 32], P('groups'), parts along dimension 0
There are 2 independent parts, one for each index of `groups`. A program takes and returns all parts, laid end to end along the dimension named above; an argument that names none is the same for every part. Nothing has to cross between parts.
All inputs are finite; a program needn't handle non-finite values.
Results may differ from a plain program's by a relative error of at most 0.015.
Values may be sent and summed in bfloat16 or wider, within the bound.
A program may use at most 448 MiB of HBM per device.

v0:
```python
import jax
import jax.numpy as jnp
from jax import lax
from jax.sharding import PartitionSpec as P


def padded_2(shard, sides, width):
    for axis, dim in sides:
        devices, length = (lax.axis_size(axis), shard.shape[dim])
        up = [(i, (i + 1) % devices) for i in range(devices - 1)]
        down = [(j, i) for i, j in up]
        last = lax.slice_in_dim(shard, length - width, length, axis=dim)
        initial = lax.slice_in_dim(shard, 0, width, axis=dim)
        before = lax.ppermute(last, axis, up)
        after = lax.ppermute(initial, axis, down)
        shard = jnp.concatenate([before, shard, after], axis=dim)
    return shard


def pad_sides(field):
    return jnp.pad(field, ((0, 0), (0, 0), (1, 1), (1, 1)))


def forward_conv(padded, kernel):
    size_x, size_y, size_z = (padded.shape[1] - 2, padded.shape[2] - 2, padded.shape[3] - 2)
    total = jnp.zeros((kernel.shape[3], size_x, size_y, size_z), jnp.float32)
    for offset in range(27):
        along_x, along_y, along_z = (offset // 9, offset // 3 % 3, offset % 3)
        window = padded[
            :, along_x : along_x + size_x, along_y : along_y + size_y, along_z : along_z + size_z
        ]
        total = total + jnp.einsum(
            "oc,cxyz->oxyz",
            kernel[along_x, along_y, along_z],
            window,
            preferred_element_type=jnp.float32,
        )
    return total


def adjoint_conv(padded, kernel):
    size_x, size_y, size_z = (padded.shape[1] - 2, padded.shape[2] - 2, padded.shape[3] - 2)
    total = jnp.zeros((kernel.shape[4], size_x, size_y, size_z), jnp.float32)
    for offset in range(27):
        along_x, along_y, along_z = (offset // 9, offset // 3 % 3, offset % 3)
        window = padded[
            :,
            2 - along_x : 2 - along_x + size_x,
            2 - along_y : 2 - along_y + size_y,
            2 - along_z : 2 - along_z + size_z,
        ]
        total = total + jnp.einsum(
            "oc,oxyz->cxyz",
            kernel[along_x, along_y, along_z],
            window,
            preferred_element_type=jnp.float32,
        )
    return total


def kernel_grad(outgrad, padded):
    size_x, size_y, size_z = (outgrad.shape[1], outgrad.shape[2], outgrad.shape[3])
    pieces = []
    for offset in range(27):
        along_x, along_y, along_z = (offset // 9, offset // 3 % 3, offset % 3)
        window = padded[
            :, along_x : along_x + size_x, along_y : along_y + size_y, along_z : along_z + size_z
        ]
        pieces.append(
            jnp.einsum("oxyz,cxyz->oc", outgrad, window, preferred_element_type=jnp.float32)
        )
    stacked = jnp.stack(pieces, axis=0)
    return stacked.reshape((3, 3, 3) + stacked.shape[1:])


def pool_sum(field):
    chans, size_x, size_y, size_z = field.shape
    return field.reshape(chans, size_x // 2, 2, size_y // 2, 2, size_z // 2, 2).sum(axis=(2, 4, 6))


def upsample(field):
    return jnp.repeat(jnp.repeat(jnp.repeat(field, 2, axis=1), 2, axis=2), 2, axis=3)


def silu_slope(value):
    sigma = jax.nn.sigmoid(value)
    return sigma * (1.0 + value * (1.0 - sigma))


def shards(inflow, speed_bin, bin_table, w_in, w_mid, w_dec, w_out, grad_pred):
    inflow_pad = pad_sides(padded_2(inflow, (("block", 1),), 1))
    onehot = (jnp.arange(bin_table.shape[0], dtype=jnp.int32) == speed_bin[0]).astype(jnp.float32)
    bias = jnp.dot(onehot, bin_table.astype(jnp.float32), precision=lax.Precision.HIGHEST)
    enc = jax.nn.relu(forward_conv(inflow_pad, w_in) + bias[:, None, None, None]).astype(
        jnp.bfloat16
    )
    pooled = (pool_sum(enc.astype(jnp.float32)) * 0.125).astype(jnp.bfloat16)
    mid_input = pad_sides(padded_2(pooled, (("block", 1),), 1))
    coarse_pre = forward_conv(mid_input, w_mid)
    coarse = jax.nn.silu(coarse_pre).astype(jnp.bfloat16)
    enc_x = padded_2(enc, (("block", 1),), 1)
    coarse_x = padded_2(coarse, (("block", 1),), 1)
    joined_x = jnp.concatenate([upsample(coarse_x)[:, 1:-1], enc_x], axis=0)
    joined_pad = pad_sides(joined_x)
    dec_pre = forward_conv(joined_pad, w_dec)
    dec = jax.nn.silu(dec_pre).astype(jnp.bfloat16)
    pred = jnp.einsum("oc,cxyz->oxyz", w_out, dec, preferred_element_type=jnp.float32)
    grad_w_out = jnp.einsum("oxyz,cxyz->oc", grad_pred, dec, preferred_element_type=jnp.float32)
    back = jnp.einsum("oc,oxyz->cxyz", w_out, grad_pred, preferred_element_type=jnp.float32)
    grad_dec = (back * silu_slope(dec_pre)).astype(jnp.bfloat16)
    grad_w_dec = kernel_grad(grad_dec, joined_pad)
    grad_pad = pad_sides(padded_2(grad_dec, (("block", 1),), 1))
    up_channels = coarse.shape[0]
    grad_up = adjoint_conv(grad_pad, w_dec[:, :, :, :, :up_channels])
    grad_coarse = (pool_sum(grad_up) * silu_slope(coarse_pre)).astype(jnp.bfloat16)
    grad_w_mid = kernel_grad(grad_coarse, mid_input)
    totals = lax.psum((grad_w_out, grad_w_dec, grad_w_mid), "block")
    return (pred, totals[0], totals[1], totals[2])


def solution(mesh):
    return jax.shard_map(
        shards,
        mesh=mesh,
        in_specs=(
            P(None, ("groups", "block"), None, None),
            P("groups"),
            P(),
            P(),
            P(),
            P(),
            P(),
            P(None, ("groups", "block"), None, None),
        ),
        out_specs=(
            P(None, ("groups", "block"), None, None),
            P("groups", None),
            P("groups", None, None, None, None),
            P("groups", None, None, None, None),
        ),
        check_vma=False,
    )
```

profile of v0, /device:TPU:0, one launch (start us, length us, event | category | flops | bytes accessed | tf_op | source)
XLA Modules:
  0.0 759.1 jit_solution(14464243881196860440)
XLA Ops:
  85.9 35.9 %fusion.20 = bf16[32,8,16,256]{3,0,2,1:T(8,128)(2,1)S(1)} fusion(f32[8,16,256,32]{2,3,1,0:T(8,128)} %fusion.264, f32[8,16,256,32]{2,3,1,0:T(8,128)} %fusion.266, f32[8,16,256,32]{2,3,1,0:T(8,128)} %fusion.268, f32[8,16,256,32]{2,3,1,0:T(8,128)} %fusion.270, f32[8,16,256,32]{2,3,1,0:T(8,128)} %fusion.272, f32[8,16,256,32]{2,3,1,0:T(8,128)} %fusion.274, ...), kind=kOutput, calls=%fused_computation.72 | convolution fusion | flops 39387136 | bytes 111445504 | tf_op jit(solution)/shard_map/oc,cxyz->oxyz/dot_general | solution.py:32
  121.8 7.5 copy.40
  129.2 13.1 %reduce_sum.18 = f32[32,4,8,128]{0,3,2,1:T(8,128)} reduce(f32[32,4,2,8,2,128,2]{0,6,5,4,3,2,1:T(2,128)} %bitcast.1492, f32[]{:T(128)} %constant.5.clone.1), dimensions={2,4,6}, to_apply=%region_0.1 | reduce | flops 917504 | bytes 4718596 | tf_op jit(solution)/shard_map/reduce_sum | solution.py:78
  144.6 5.2 collective-permute-start.2
  166.2 4.9 collective-permute-start.4
  181.4 4.5 broadcast_in_dim.11
  185.9 5.5 broadcast_in_dim.12
  191.4 9.8 %slice.1053 = bf16[64,10,16,256]{0,2,3,1:T(8,128)(2,1)} slice(bf16[64,12,16,256]{0,2,3,1:T(8,128)(2,1)} %bitcast.1493), slice={[0:64], [1:11], [0:16], [0:256]} | slice | bytes 10485760 | tf_op jit(solution)/shard_map/slice | solution.py:103
  201.2 12.6 %copy.213 = bf16[64,10,16,256]{3,0,2,1:T(8,128)(2,1)} copy(bf16[64,10,16,256]{0,2,3,1:T(8,128)(2,1)} %slice.1053) | data formatting | bytes 10485760
  213.8 4.1 maximum_maximum_fusion
  236.5 3.9 fusion.38
  265.1 4.2 fusion.54
  279.6 3.9 fusion.62
  302.9 32.6 %multiply_convert_fusion.1 = (bf16[32,8,16,256]{3,0,2,1:T(8,128)(2,1)}, f32[32,8,16,256]{3,0,2,1:T(8,128)}) fusion(bf16[96,10,16,256]{3,0,2,1:T(8,128)(2,1)S(1)} %maximum_maximum_fusion, bf16[3,3,3,32,96]{4,3,2,1,0:T(8,128)(2,1)S(1)} %copy-done.7, f32[8,16,256,32]{2,3,1,0:T(8,128)} %fusion.66, f32[8,16,256,32]{2,3,1,0:T(8,128)} %fusion.64, ...), kind=kOutput, calls=%fused_computation.87 | convolution fusion | flops 233832448 | bytes 123215872 | tf_op jit(solution)/shard_map/oc,cxyz->oxyz/dot_general | solution.py:32
  335.5 4.0 multiply_convert_fusion
  342.2 4.6 fusion.384
  410.4 5.5 collective-permute-start.8
  420.5 4.6 select_maximum_fusion
  425.1 4.6 fusion.78
  429.8 4.6 fusion.80
  434.4 4.6 fusion.82
  438.9 4.6 fusion.84
  443.5 4.5 fusion.86
  448.0 4.6 fusion.88
  452.6 4.6 fusion.90
  457.2 4.5 fusion.92
  461.7 4.6 fusion.94
  466.4 5.0 fusion.96
  471.4 4.6 fusion.98
  476.0 4.6 fusion.100
  480.6 4.5 fusion.102
  485.1 4.6 fusion.104
  489.8 4.5 fusion.106
  494.3 4.6 fusion.108
  498.9 4.6 fusion.110
  503.4 4.6 fusion.112
  508.1 4.5 fusion.114
  512.6 4.7 fusion.116
  517.3 4.5 fusion.118
  521.9 4.6 fusion.120
  526.4 4.6 fusion.122
  531.0 4.5 fusion.73
  535.5 4.5 fusion.69
  540.1 69.2 %bitcast_add_fusion = f32[64,8,16,256]{3,0,2,1:T(8,128)} fusion(f32[8,16,256,64]{2,3,1,0:T(8,128)} %fusion.78, f32[8,16,256,64]{2,3,1,0:T(8,128)} %fusion.80, f32[8,16,256,64]{2,3,1,0:T(8,128)} %fusion.82, f32[8,16,256,64]{2,3,1,0:T(8,128)} %fusion.73, f32[8,16,256,64]{2,3,1,0:T(8,128)} %fusion.84, f32[8,16,256,64]{2,3,1,0:T(8,128)} %fusion.86, ...), kind=kOutput, calls=%fused_computation.31 | convolution fusion | flops 188743680 | bytes 228597760 | tf_op jit(solution)/shard_map/oc,oxyz->cxyz/dot_general | solution.py:52
  609.3 12.2 %copy.46 = f32[64,8,16,256]{0,3,2,1:T(8,128)} copy(f32[64,8,16,256]{3,0,2,1:T(8,128)} %bitcast_add_fusion) | data formatting | bytes 16777216 | tf_op jit(solution)/shard_map/add | solution.py:52
  621.5 13.3 %reduce_sum.19 = f32[64,4,8,128]{0,3,2,1:T(8,128)} reduce(f32[64,4,2,8,2,128,2]{0,6,5,4,3,2,1:T(2,128)} %bitcast.1491, f32[]{:T(128)} %constant.5.clone.1), dimensions={2,4,6}, to_apply=%region_3.4 | reduce | flops 1835008 | bytes 9437188 | tf_op jit(solution)/shard_map/reduce_sum | solution.py:78
  651.2 35.9 %psum.21 = f32[4,32]{1,0:T(4,128)} all-reduce(f32[4,32]{1,0:T(4,128)S(1)} %convolution_bitcast_fusion.38), channel_id=1, replica_groups=mesh['groups'=2,'block'=16] {'block'}, use_global_device_ids=true, to_apply=%region_1.2 | all-reduce | flops 128 | bytes 1024 | tf_op jit(solution)/shard_map/psum | solution.py:117
  687.1 61.3 %all-reduce.7.cloned.1.call-done = (f32[3,3,3,32,96]{4,3,2,1,0:T(8,128)}, f32[3,3,3,64,32]{3,4,2,1,0:T(8,128)}) async-done(((f32[3,3,3,32,96]{4,3,2,1,0:T(8,128)}, f32[3,3,3,64,32]{3,4,2,1,0:T(8,128)}), (f32[3,3,3,32,96]{4,3,2,1,0:T(8,128)}, f32[3,3,3,64,32]{3,4,2,1,0:T(8,128)})) %all-reduce.7.cloned.1.call-update) | async-done | bytes 552976 | tf_op jit(solution)/shard_map/psum | solution.py:117
  (208 shorter events, 270.5 us)
Async XLA Ops:
  7.2 328.3 %copy-start = (bf16[4,8,16,256]{3,2,1,0:T(8,128)(2,1)S(1)}, bf16[4,8,16,256]{3,2,1,0:T(8,128)(2,1)}, u32[]{:S(2)}) copy-start(bf16[4,8,16,256]{3,2,1,0:T(8,128)(2,1)} %param.15) | copy-start | bytes 786436
  7.2 10.0 %copy-start.15 = (bf16[3,3,3,32,4]{3,4,2,1,0:T(4,128)(2,1)S(1)}, bf16[3,3,3,32,4]{3,4,2,1,0:T(4,128)(2,1)}, u32[]{:S(2)}) copy-start(bf16[3,3,3,32,4]{3,4,2,1,0:T(4,128)(2,1)} %param.11) | copy-start | bytes 20740
  7.2 9.4 %copy-start.16 = (bf16[16,32]{1,0:T(8,128)(2,1)S(1)}, bf16[16,32]{1,0:T(8,128)(2,1)}, u32[]{:S(2)}) copy-start(bf16[16,32]{1,0:T(8,128)(2,1)} %param.10) | copy-start | bytes 3076
  7.2 741.2 %all-reduce.7.cloned.1.call-start = ((), (), s32[]{:S(2)}) async-start(), calls=%async_computation | async-start | bytes 1769472 | tf_op jit(solution)/shard_map/psum | solution.py:117
  8.5 8.2 %collective-permute-start = (bf16[4,1,16,256]{3,0,2,1:T(4,128)(2,1)S(1)}, bf16[4,1,16,256]{3,0,2,1:T(4,128)(2,1)S(1)}, u32[]{:S(2)}, u32[]{:S(2)}) collective-permute-start(bf16[4,1,16,256]{3,0,2,1:T(4,128)(2,1)S(1)} %get-tuple-element.26), channel_id=1, source_target_pairs={{0,1},{1,2},{2,3},{3,4},{4,5},{5,6},{6,7},{7,8},{8,9},{9,10},{10,1... | collective-permute-start | bytes 98312 | tf_op jit(solution)/shard_map/ppermute | solution.py:14
  10.8 5.9 collective-permute-start.1
  142.3 12.3 %copy-start.14 = (bf16[3,3,3,64,32]{3,4,2,1,0:T(8,128)(2,1)S(1)}, bf16[3,3,3,64,32]{3,4,2,1,0:T(8,128)(2,1)}, u32[]{:S(2)}) copy-start(bf16[3,3,3,64,32]{3,4,2,1,0:T(8,128)(2,1)} %param.12) | copy-start | bytes 331780
  144.6 19.7 %copy-start.4 = (bf16[32,4,8,128]{3,0,2,1:T(8,128)(2,1)}, bf16[32,4,8,128]{3,0,2,1:T(8,128)(2,1)S(1)}, u32[]{:S(2)}) copy-start(bf16[32,4,8,128]{3,0,2,1:T(8,128)(2,1)S(1)} %multiply_convert_fusion.4) | copy-start | bytes 786436
  144.6 6.7 collective-permute-start.2
  149.8 4.4 collective-permute-start.3
  151.3 10.2 %copy-start.12 = (bf16[32,1,8,128]{3,0,2,1:T(8,128)(2,1)}, bf16[32,1,8,128]{3,0,2,1:T(8,128)(2,1)S(1)}, u32[]{:S(2)}) copy-start(bf16[32,1,8,128]{3,0,2,1:T(8,128)(2,1)S(1)} %collective-permute-done.2) | copy-start | bytes 196612
  154.2 10.1 %copy-start.10 = (bf16[32,1,8,128]{3,0,2,1:T(8,128)(2,1)}, bf16[32,1,8,128]{3,0,2,1:T(8,128)(2,1)S(1)}, u32[]{:S(2)}) copy-start(bf16[32,1,8,128]{3,0,2,1:T(8,128)(2,1)S(1)} %collective-permute-done.3) | copy-start | bytes 196612
  154.6 10.1 %copy-start.2 = (bf16[32,6,10,130]{3,0,2,1:T(8,128)(2,1)}, bf16[32,6,10,130]{3,0,2,1:T(8,128)(2,1)S(1)}, u32[]{:S(2)}) copy-start(bf16[32,6,10,130]{3,0,2,1:T(8,128)(2,1)S(1)} %select_maximum_fusion.2) | copy-start | bytes 1497604
  166.2 11.3 %collective-permute-start.4 = (bf16[64,1,8,128]{3,0,2,1:T(8,128)(2,1)S(1)}, bf16[64,1,8,128]{3,0,2,1:T(8,128)(2,1)S(1)}, u32[]{:S(2)}, u32[]{:S(2)}) collective-permute-start(bf16[64,1,8,128]{3,0,2,1:T(8,128)(2,1)S(1)} %get-tuple-element.22), channel_id=1, source_target_pairs={{0,1},{1,2},{2,3},{3,4},{4,5},{5,6},{6,7},{7,8},{8,9},{9,10},{10,1... | collective-permute-start | bytes 393224 | tf_op jit(solution)/shard_map/ppermute | solution.py:14
  171.1 6.5 collective-permute-start.5
  173.2 40.5 %collective-permute-start.6 = (bf16[32,1,16,256]{3,0,2,1:T(8,128)(2,1)}, bf16[32,1,16,256]{3,0,2,1:T(8,128)(2,1)S(1)}, u32[]{:S(2)}, u32[]{:S(2)}) collective-permute-start(bf16[32,1,16,256]{3,0,2,1:T(8,128)(2,1)} %get-tuple-element.20), channel_id=1, source_target_pairs={{0,1},{1,2},{2,3},{3,4},{4,5},{5,6},{6,7},{7,8},{8,9},{9,10},{10,1... | collective-permute-start | bytes 786440 | tf_op jit(solution)/shard_map/ppermute | solution.py:14
  176.3 37.5 %collective-permute-start.7 = (bf16[32,1,16,256]{3,0,2,1:T(8,128)(2,1)}, bf16[32,1,16,256]{3,0,2,1:T(8,128)(2,1)}, u32[]{:S(2)}, u32[]{:S(2)}) collective-permute-start(bf16[32,1,16,256]{3,0,2,1:T(8,128)(2,1)} %get-tuple-element.21), channel_id=1, source_target_pairs={{1,0},{2,1},{3,2},{4,3},{5,4},{6,5},{7,6},{8,7},{9,8},{10,9},{11,1... | collective-permute-start | bytes 786440 | tf_op jit(solution)/shard_map/ppermute | solution.py:15
  213.8 4.2 copy-start.7
  302.9 32.6 %copy-start.17 = (bf16[4,32]{1,0:T(4,128)(2,1)S(1)}, bf16[4,32]{1,0:T(4,128)(2,1)}, u32[]{:S(2)}) copy-start(bf16[4,32]{1,0:T(4,128)(2,1)} %param.14) | copy-start | bytes 772
  410.4 9.5 %collective-permute-start.8 = (bf16[32,1,16,256]{3,0,2,1:T(8,128)(2,1)S(1)}, bf16[32,1,16,256]{3,0,2,1:T(8,128)(2,1)S(1)}, u32[]{:S(2)}, u32[]{:S(2)}) collective-permute-start(bf16[32,1,16,256]{3,0,2,1:T(8,128)(2,1)S(1)} %get-tuple-element.18), channel_id=1, source_target_pairs={{0,1},{1,2},{2,3},{3,4},{4,5},{5,6},{6,7},{7,8},{8,9},{9,10},{10,1... | collective-permute-start | bytes 786440 | tf_op jit(solution)/shard_map/ppermute | solution.py:14
  415.8 4.7 collective-permute-start.9
  419.8 10.0 %copy-start.8 = (f32[27,32,96]{2,1,0:T(8,128)}, f32[27,32,96]{2,1,0:T(8,128)S(1)}, u32[]{:S(2)}) copy-start(f32[27,32,96]{2,1,0:T(8,128)S(1)} %fusion.147) | copy-start | bytes 995332
  425.1 101.3 %copy-start.1 = (bf16[32,10,18,258]{3,0,2,1:T(8,128)(2,1)}, bf16[32,10,18,258]{3,0,2,1:T(8,128)(2,1)S(1)}, u32[]{:S(2)}) copy-start(bf16[32,10,18,258]{3,0,2,1:T(8,128)(2,1)S(1)} %select_maximum_fusion) | copy-start | bytes 8916484
  634.8 3.9 copy-start.3
  634.8 5.1 copy-start.5
  634.8 5.1 copy-start.13
  642.1 3.3 copy-start.11
  643.9 3.9 copy-start.18
  645.7 4.9 copy-start.6
  646.9 0.8 copy-start.9
Sparse Core Ops, SparseCore 0:
  647.8 100.5 all-reduce.6
where the time goes:
time: 769 us; the launch traced here: 759 us
  matrix products  510 us (66%)
  local copies, waits for them, and re-layouts  67.8 us (9%)
  waiting for transfers between devices  64.9 us (8%)
  other arithmetic  37.8 us (5%)
  blocking collectives  35.9 us (5%)
  starting transfers between devices  27.6 us (4%)
  between operations  15.6 us (2%)
    dot_general x81, matrix products, forward_conv(): jnp.einsum('oc,cxyz->oxyz', kernel[along_x, along_y, along_z], window, pr...  237 us
    dot_general x27, matrix products, adjoint_conv(): jnp.einsum('oc,oxyz->cxyz', kernel[along_x, along_y, along_z], window, pr...  189 us
    dot_general x54, matrix products, kernel_grad(): jnp.einsum('oxyz,cxyz->oc', outgrad, window, preferred_element_type=jnp.f...  76.9 us
    psum x1, waiting for transfers between devices, shards(): totals = lax.psum((grad_w_out, grad_w_dec, grad_w_mid), 'block')  61.3 us
    psum x1, blocking collectives, shards(): totals = lax.psum((grad_w_out, grad_w_dec, grad_w_mid), 'block')  35.9 us
    reduce_sum x2, other arithmetic, pool_sum(): field.reshape(chans, size_x // 2, 2, size_y // 2, 2, size_z // 2, 2)  26.4 us
    ppermute x5, starting transfers between devices, padded_2(): before = lax.ppermute(last, axis, up)  20.9 us
    unnamed x43, local copies, waits for them, and re-layouts  19.2 us
  transfers between devices with their start and end apart: 11, of which 3 were waited for; matrix products, arithmetic and copies ran while one was open for 6% of the time, Pallas kernels for 0%

commit v1 on v0

v1 whole, which is shorter than its diff:
```python
import jax
import jax.numpy as jnp
import numpy as np
from jax import lax
from jax.experimental import pallas as pl
from jax.experimental.pallas import tpu as pltpu
from jax.sharding import PartitionSpec as P

F32, BF16 = jnp.float32, jnp.bfloat16
LANES = 128
YC = 8
CELLS = YC * LANES
WIDE = CELLS + 2 * LANES
WINDOW = ((1, 0), (0, LANES), (1, LANES), (0, 2 * LANES))
PARITIES = tuple((p // 4, p // 2 % 2, p % 2) for p in range(8))


def place_tables():
    fine = np.zeros((2, 3, 4), np.float32)
    coarse = np.zeros((2, 3, 3), np.float32)
    child = np.zeros((3, 4), np.float32)
    for p in range(2):
        for a in range(3):
            fine[p, a, p + a] = 1
            coarse[p, a, (p + a - 1) // 2 + 1] = 1
            child[a, p + 2 - a] += 1
    t_in = np.einsum("pax,qby,rez->pqrabexzy", fine, fine, fine).reshape(8, 27, 64)
    t_skip = np.einsum("pax,qby,rez->pqrabeyxz", fine, fine, fine).reshape(8, 27, 64)
    t_up = np.einsum("pax,qby,rez->pqrabeyxz", coarse, coarse, coarse).reshape(8, 27, 27)
    t_adj = np.einsum("ax,by,ez->abeyxz", child, child, child).reshape(27, 64)
    order = np.zeros((8, 8), np.float32)
    for i, (px, py, pz) in enumerate(PARITIES):
        order[i, px * 4 + pz * 2 + py] = 1
    split = np.zeros((256, 512), np.float32)
    merge = np.zeros((256, 256), np.float32)
    for z in range(LANES):
        for w in range(4):
            if 0 <= 2 * z - 1 + w < 256:
                split[2 * z - 1 + w, w * LANES + z] = 1
        for p in range(2):
            merge[p * LANES + z, 2 * z + p] = 1
    return t_in, t_skip, t_up, t_adj, order, split, merge


def dot(a, b):
    return jnp.dot(a, b, preferred_element_type=F32)


def shifted(v, by):
    z = lax.broadcasted_iota(jnp.int32, v.shape, 1) % LANES
    if by == 1:
        return jnp.where(z == 0, 0.0, pltpu.roll(v, 1, 1))
    return jnp.where(z == LANES - 1, 0.0, pltpu.roll(v, v.shape[1] - 1, 1))


def row(start, size, unit):
    return pl.ds(pl.multiple_of(start * unit, unit), size)


def put_fine(ref, par, line, low, high):
    block = jnp.concatenate([shifted(high, 1), low, high, shifted(low, -1)], axis=0)
    ref[par, row(line, 128, 128), LANES : LANES + CELLS] = block.astype(BF16)


def put_coarse(ref, plane, v):
    block = jnp.concatenate([shifted(v, 1), v, shifted(v, -1)], axis=0)
    n = 3 * v.shape[0]
    ref[row(plane, n, n), LANES : LANES + CELLS] = block.astype(BF16)


def rows_to_lanes(v, first, count, lane):
    return jnp.concatenate(
        [v[8 * y + first : 8 * y + first + count, lane : lane + LANES] for y in range(YC)], axis=1
    )


def body(
    edge, before, inflow, after, gp, bias, w_in, w_mid, w_skip, w_up, w_adj, w_back, w_pred,
    split, merge,
    pred, g_out, g_skip, g_up, g_mid,
    patch, gpatch, enc_s, pool_s, coarse_s, pre_s, gd_s, gt_s, gct_s, acc_s,
):
    first, last = edge[0] == 1, edge[1] == 1
    for ref in (enc_s, gd_s):
        ref[:, :, 0:LANES] = jnp.zeros(ref.shape[:2] + (LANES,), BF16)
        ref[:, :, LANES + CELLS :] = jnp.zeros(ref.shape[:2] + (LANES,), BF16)
    for ref in (pool_s, coarse_s):
        ref[:, 0:LANES] = jnp.zeros((ref.shape[0], LANES), BF16)
        ref[:, LANES + CELLS :] = jnp.zeros((ref.shape[0], LANES), BF16)
    coarse_s[0:192, :] = jnp.zeros((192, WIDE), BF16)
    coarse_s[7 * 192 : 8 * 192, :] = jnp.zeros((192, WIDE), BF16)
    g_out[...] = jnp.zeros(g_out.shape, F32)

    def put_inflow(line, value):
        parts = dot(value, split[...])
        block = [rows_to_lanes(parts, 0, 16, w * LANES) for w in range(4)]
        patch[row(line, 64, 64), :] = jnp.concatenate(block, axis=0).astype(BF16)

    def put_gp(line, value):
        parts = dot(value, split[:, LANES : 3 * LANES])
        block = [rows_to_lanes(parts, 0, 8, w * LANES) for w in range(2)]
        gpatch[row(line, 16, 16), :] = jnp.concatenate(block, axis=0).astype(BF16)

    def edges(i, c):
        put_inflow(i, before[i])
        put_inflow(i + 13, after[i])
        return c

    def middle(i, c):
        put_inflow(i + 5, inflow[i])
        put_gp(i + 1, gp[i][4:68])
        return c

    lax.fori_loop(0, 5, edges, 0)
    lax.fori_loop(0, 8, middle, 0)
    put_gp(0, before[5][4:68])
    put_gp(9, after[5][4:68])

    def encode(xe, c):
        outside = (first & (xe < 2)) | (last & (xe > 5))
        v = dot(w_in[...], patch[row(xe, 256, 128), :]) + bias[...]
        v = jnp.where(outside, 0.0, jnp.maximum(v, 0.0)).astype(BF16).astype(F32)
        total = v[0:32]
        for p in range(1, 8):
            total = total + v[p * 32 : p * 32 + 32]
        put_coarse(pool_s, xe, total * 0.125)
        for px in range(2):
            for py in range(2):
                at = (px * 2 + py) * 64
                put_fine(enc_s, py, 2 * xe + px, v[at : at + 32], v[at + 32 : at + 64])
        return c

    lax.fori_loop(0, 8, encode, 0)

    def middle_level(xk, c):
        pre = jnp.zeros((64, CELLS), F32)
        for dy in range(3):
            pre = pre + dot(
                w_mid[:, dy * 288 : dy * 288 + 288],
                pool_s[row(xk, 288, 96), dy * LANES : dy * LANES + CELLS],
            )
        pre_s[xk] = pre
        outside = (first & (xk < 1)) | (last & (xk > 4))
        put_coarse(coarse_s, xk + 1, jnp.where(outside, 0.0, pre * jax.nn.sigmoid(pre)))
        return c

    lax.fori_loop(0, 6, middle_level, 0)

    def decode_pre(xc, rows):
        v = jnp.zeros((rows[1] - rows[0], CELLS), F32)
        for yw, (par, start) in enumerate(WINDOW):
            v = v + dot(
                w_skip[rows[0] : rows[1], yw * 512 : yw * 512 + 512],
                enc_s[par, row(2 * xc + 3, 512, 128), start : start + CELLS],
            )
        for dy in range(3):
            v = v + dot(
                w_up[rows[0] : rows[1], dy * 576 : dy * 576 + 576],
                coarse_s[row(xc + 1, 576, 192), dy * LANES : dy * LANES + CELLS],
            )
        return v

    def put_grad(xc, pxs, grad):
        for i, px in enumerate(pxs):
            for py in range(2):
                at = (i * 2 + py) * 64
                put_fine(gd_s, py, 2 * xc + px + 1, grad[at : at + 32], grad[at + 32 : at + 64])

    def decode(xc, c):
        v = decode_pre(xc, (0, 256))
        sigma = jax.nn.sigmoid(v)
        dec = (v * sigma).astype(BF16)
        cot = gpatch[row(2 * xc + 1, 32, 16), :]
        grad = dot(w_back[...], cot) * (sigma * (1.0 + v * (1.0 - sigma)))
        out = dot(w_pred[...], dec)
        for px in range(2):
            halves = []
            for pz in range(2):
                at = (px * 2 + pz) * 8
                halves.append(
                    jnp.concatenate(
                        [out[at : at + 8, y * LANES : y * LANES + LANES] for y in range(YC)],
                        axis=0,
                    )
                )
            line = jnp.concatenate(halves, axis=1)
            high = line.astype(BF16)
            low = (line - high.astype(F32)).astype(BF16)
            pred[2 * xc + px] = dot(high, merge[...]) + dot(low, merge[...])
        full = lax.dot_general(cot, dec, (((1,), (1,)), ((), ())), preferred_element_type=F32)
        for i, (px, py, pz) in enumerate(PARITIES):
            at = (px * 4 + pz * 2 + py) * 4
            g_out[...] += full[at : at + 4, i * 32 : i * 32 + 32]
        put_grad(xc, (0, 1), grad)
        gt_s[row(xc, CELLS, CELLS), :] = grad.T.astype(BF16)
        return c

    def rim(xc, px, line):
        v = decode_pre(xc, (px * 128, px * 128 + 128))
        sigma = jax.nn.sigmoid(v)
        back = dot(
            w_back[px * 128 : px * 128 + 128, px * 16 : px * 16 + 16],
            gpatch[line * 16 : line * 16 + 16, :],
        )
        put_grad(xc, (px,), back * (sigma * (1.0 + v * (1.0 - sigma))))

    rim(-1, 1, 0)
    rim(4, 0, 9)
    lax.fori_loop(0, 4, decode, 0)

    def coarse_grad(xc, c):
        v = jnp.zeros((64, CELLS), F32)
        for yw, (par, start) in enumerate(WINDOW):
            v = v + dot(
                w_adj[:, yw * 512 : yw * 512 + 512],
                gd_s[par, row(xc, 512, 256), start : start + CELLS],
            )
        pre = pre_s[xc + 1]
        sigma = jax.nn.sigmoid(pre)
        v = v * (sigma * (1.0 + pre * (1.0 - sigma)))
        gct_s[row(xc, CELLS, CELLS), :] = v.T.astype(BF16)
        return c

    lax.fori_loop(0, 4, coarse_grad, 0)

    for dy in range(3):
        total = jnp.zeros((288, 64), F32)
        for xc in range(4):
            total = total + dot(
                pool_s[(xc + 1) * 96 : (xc + 1) * 96 + 288, dy * LANES : dy * LANES + CELLS],
                gct_s[xc * CELLS : (xc + 1) * CELLS, :],
            )
        g_mid[dy] = total
    for yw, (par, start) in enumerate(WINDOW):
        total = jnp.zeros((512, 256), F32)
        for xc in range(4):
            total = total + dot(
                enc_s[par, (2 * xc + 3) * 128 : (2 * xc + 7) * 128, start : start + CELLS],
                gt_s[xc * CELLS : (xc + 1) * CELLS, :],
            )
        acc_s[yw * 512 : yw * 512 + 512, :] = total
    for a in range(3):
        for b in range(3):
            total = jnp.zeros((96, 32), F32)
            for i, (px, py, pz) in enumerate(PARITIES):
                at = (py + b) * 512 + (px + a) * 128 + pz * 32
                total = total + acc_s[at : at + 96, i * 32 : i * 32 + 32]
            g_skip[a, b] = total
    for dy in range(3):
        total = jnp.zeros((576, 256), F32)
        for xc in range(4):
            total = total + dot(
                coarse_s[(xc + 1) * 192 : (xc + 4) * 192, dy * LANES : dy * LANES + CELLS],
                gt_s[xc * CELLS : (xc + 1) * CELLS, :],
            )
        acc_s[dy * 576 : dy * 576 + 576, :] = total
    for a in range(3):
        for b in range(3):
            for e in range(3):
                total = jnp.zeros((64, 32), F32)
                for i, (px, py, pz) in enumerate(PARITIES):
                    dx, dy, dz = (px + a + 1) // 2, (py + b + 1) // 2, (pz + e + 1) // 2
                    at = dy * 576 + dx * 192 + dz * 64
                    total = total + acc_s[at : at + 64, i * 32 : i * 32 + 32]
                g_up[a, b, e] = total


def shards(inflow, speed_bin, bin_table, w_in, w_mid, w_dec, w_out, grad_pred):
    t_in, t_skip, t_up, t_adj, order, split, merge = (
        jnp.asarray(t, BF16) for t in place_tables()
    )
    lines = lambda f: jnp.pad(
        f.transpose(1, 2, 0, 3).reshape(f.shape[1], 64, 256), ((0, 0), (4, 4), (0, 0))
    )
    field, cot = lines(inflow), lines(grad_pred)
    devices = lax.axis_size("block")
    up = [(i, i + 1) for i in range(devices - 1)]
    down = [(i + 1, i) for i in range(devices - 1)]
    before = lax.ppermute(jnp.concatenate([field[3:8], cot[7:8]], axis=0), "block", up)
    after = lax.ppermute(jnp.concatenate([field[0:5], cot[0:1]], axis=0), "block", down)
    me = lax.axis_index("block")
    edge = jnp.stack([me == 0, me == devices - 1]).astype(jnp.int32)
    bias = jnp.tile(lax.dynamic_index_in_dim(bin_table, speed_bin[0], 0, False), 8)
    bias = bias.astype(F32)[:, None]
    spread = lambda t, w: (
        jnp.einsum("PkD,koc->PoDc", t, w.reshape((27,) + w.shape[3:]), preferred_element_type=F32)
        .astype(BF16)
        .reshape(256, -1)
    )
    k_in = spread(t_in, w_in)
    k_skip = spread(t_skip, w_dec[..., 64:])
    k_up = spread(t_up, w_dec[..., :64])
    k_mid = w_mid.transpose(3, 1, 0, 2, 4).reshape(64, 864)
    k_adj = (
        jnp.einsum(
            "kD,koc->cDo", t_adj, w_dec[..., :64].reshape(27, 32, 64), preferred_element_type=F32
        )
        .astype(BF16)
        .reshape(64, 2048)
    )
    k_back = (order[:, None, :, None] * w_out.T[None, :, None, :]).reshape(256, 32)
    k_pred = k_back.T
    vmem = pl.BlockSpec(memory_space=pltpu.VMEM)
    shape = jax.ShapeDtypeStruct
    pred, g_out, g_skip, g_up, g_mid = pl.pallas_call(
        body,
        out_shape=(
            shape((8, 64, 256), F32),
            shape((4, 32), F32),
            shape((3, 3, 96, 32), F32),
            shape((3, 3, 3, 64, 32), F32),
            shape((3, 288, 64), F32),
        ),
        in_specs=[pl.BlockSpec(memory_space=pltpu.SMEM)] + [vmem] * 14,
        out_specs=[vmem] * 5,
        scratch_shapes=[
            pltpu.VMEM((18 * 64, CELLS), BF16),
            pltpu.VMEM((10 * 16, CELLS), BF16),
            pltpu.VMEM((2, 16 * 128, WIDE), BF16),
            pltpu.VMEM((8 * 96, WIDE), BF16),
            pltpu.VMEM((8 * 192, WIDE), BF16),
            pltpu.VMEM((6, 64, CELLS), F32),
            pltpu.VMEM((2, 10 * 128, WIDE), BF16),
            pltpu.VMEM((4 * CELLS, 256), BF16),
            pltpu.VMEM((4 * CELLS, 64), BF16),
            pltpu.VMEM((2048, 256), F32),
        ],
        compiler_params=pltpu.CompilerParams(vmem_limit_bytes=56 * 1024 * 1024),
    )(
        edge, before, field, after, cot, bias, k_in, k_mid, k_skip, k_up, k_adj, k_back, k_pred,
        split, merge,
    )
    flat = jnp.concatenate(
        [g_skip.reshape(-1), g_up.reshape(-1), g_mid.reshape(-1), g_out.reshape(-1)]
    ).reshape(-1, 128)
    flat = lax.psum(flat, "block").reshape(-1)
    ends = np.cumsum([27648, 55296, 55296, 128])
    s_skip, s_up, s_mid, s_out = (
        flat[e - n : e] for e, n in zip(ends, (27648, 55296, 55296, 128))
    )
    grad_w_dec = jnp.concatenate(
        [s_up.reshape(3, 3, 3, 64, 32), s_skip.reshape(3, 3, 3, 32, 32)], axis=3
    ).swapaxes(3, 4)
    grad_w_mid = s_mid.reshape(3, 3, 3, 32, 64).transpose(1, 0, 2, 4, 3)
    pred = pred.reshape(8, 16, 4, 256).transpose(2, 0, 1, 3)
    return (pred, s_out.reshape(4, 32), grad_w_dec, grad_w_mid)


def solution(mesh):
    return jax.shard_map(
        shards,
        mesh=mesh,
        in_specs=(
            P(None, ("groups", "block"), None, None),
            P("groups"),
            P(),
            P(),
            P(),
            P(),
            P(),
            P(None, ("groups", "block"), None, None),
        ),
        out_specs=(
            P(None, ("groups", "block"), None, None),
            P("groups", None),
            P("groups", None, None, None, None),
            P("groups", None, None, None, None),
        ),
        check_vma=False,
    )
```

time: 769 us -> 203 us (0.26); the launches traced: 759 us -> 202 us
  matrix products: 510 us -> 3.25 us
  Pallas kernels: 0 us -> 46.7 us
  blocking collectives: 35.9 us -> 0 us
  local copies, waits for them, and re-layouts: 67.8 us -> 34.5 us
  other arithmetic: 37.8 us -> 4.64 us
  waiting for transfers between devices: 64.9 us -> 93.7 us
  starting transfers between devices: 27.6 us -> 4.37 us
    dot_general x166 -> x4, matrix products: 510 us -> 3.25 us  [the longest x3 2.92 us: shards(): jnp.einsum('PkD,koc->PoDc', t, w.reshape((27,) + w.shape[3:]), preferred_...]
    pallas_call x0 -> x1, Pallas kernels: none -> 46.7 us  [shards(): pl.pallas_call(body, out_shape=(shape((8, 64, 256), F32), shape((4, 32),...]
    psum x1 -> x0, blocking collectives: 35.9 us -> none  [shards(): totals = lax.psum((grad_w_out, grad_w_dec, grad_w_mid), 'block')]
    psum x1, waiting for transfers between devices: 61.3 us -> 93.7 us  [shards(): flat = lax.psum(flat, 'block').reshape(-1)]
    reduce_sum x2 -> x0, other arithmetic: 26.4 us -> none  [pool_sum(): field.reshape(chans, size_x // 2, 2, size_y // 2, 2, size_z // 2, 2)]
    ppermute x10 -> x2, starting transfers between devices: 27.6 us -> 4.33 us  [the longest x1 3.05 us: shards(): lax.ppermute(jnp.concatenate([field[3:8], cot[7:8]], axis=0), 'block', up)]
    unnamed x43 -> x23, local copies, waits for them, and re-layouts: 19.2 us -> 0.85 us
    reshape x1 -> x22, local copies, waits for them, and re-layouts: 7.5 us -> 19.9 us  [the longest x4 10.3 us: shards(): spread = lambda t, w: jnp.einsum('PkD,koc->PoDc', t, w.reshape((27,) + w....]
  transfers between devices with their start and end apart: 11 -> 3, of which waited for: 3 -> 1; matrix products, arithmetic and copies ran while one was open for 6% -> 14% of each run, Pallas kernels for 0% -> 0%
where the time goes in v1:
time: 203 us; the launch traced here: 202 us
  waiting for transfers between devices  93.7 us (46%)
  Pallas kernels  46.7 us (23%)
  local copies, waits for them, and re-layouts  34.5 us (17%)
  between operations  14.9 us (7%)
  other arithmetic  4.64 us (2%)
  starting transfers between devices  4.37 us (2%)
  matrix products  3.25 us (2%)
    psum x1, waiting for transfers between devices, shards(): flat = lax.psum(flat, 'block').reshape(-1)  93.7 us
    pallas_call x1, Pallas kernels, shards(): pl.pallas_call(body, out_shape=(shape((8, 64, 256), F32), shape((4, 32),...  46.7 us
    reshape x4, local copies, waits for them, and re-layouts, shards(): spread = lambda t, w: jnp.einsum('PkD,koc->PoDc', t, w.reshape((27,) + w....  10.3 us
  transfers between devices with their start and end apart: 3, of which 1 were waited for; matrix products, arithmetic and copies ran while one was open for 14% of the time, Pallas kernels for 0%

profile of v1, /device:TPU:0, one launch (start us, length us, event | category | flops | bytes accessed | tf_op | source)
XLA Modules:
  0.0 202.0 jit_solution(6314479867139758342)
XLA Ops:
  7.2 1.2 copy.49
  8.5 1.2 copy.48
  9.9 0.7 pad_maximum_fusion
  10.6 3.1 %collective-permute-start = (bf16[6,72,256]{2,1,0:T(8,128)(2,1)}, bf16[6,72,256]{2,1,0:T(8,128)(2,1)}, u32[]{:S(2)}, u32[]{:S(2)}) collective-permute-start(bf16[6,72,256]{2,1,0:T(8,128)(2,1)} %pad_maximum_fusion), channel_id=1, source_target_pairs={{0,1},{1,2},{2,3},{3,4},{4,5},{5,6},{6,7},{7,8},{8,9},{9,10},{10,1... | collective-permute-start | bytes 663560 | tf_op jit(solution)/shard_map/ppermute | solution.py:279
  13.6 0.7 pad_maximum_fusion.1
  14.3 1.3 collective-permute-start.1
  15.6 0.8 pad.7.inflow
  16.4 0.8 pad.8.gp
  18.0 0.1 slice.39
  18.1 0.4 copy.53
  18.5 2.0 %convert_bitcast_fusion = bf16[8,32,27,64]{3,2,1,0:T(8,128)(2,1)} fusion(bf16[8,27,27,1]{1,2,3,0:T(8,128)(2,1)S(1)} %copy-done.5, bf16[27,32,64]{2,1,0:T(8,128)(2,1)S(1)} %bitcast.73), kind=kOutput, calls=%fused_computation | convolution fusion | flops 24330240 | bytes 1006992 | tf_op jit(solution)/shard_map/PkD,koc->PoDc/dot_general | solution.py:286
  20.6 0.3 fusion
  20.9 0.2 fusion.1
  21.1 0.7 convert_bitcast_fusion.1
  21.9 0.7 bitcast_convert_fusion
  22.6 0.8 convert_element_type.64.bias
  23.4 0.8 copy.51
  24.2 0.4 reshape.100
  24.5 0.8 copy.59.w_in
  25.3 0.9 copy.52
  26.2 0.8 copy.60.w_mid
  27.0 3.2 %copy.54 = bf16[8,32,64,32]{3,2,1,0:T(8,128)(2,1)} copy(bf16[8,32,64,32]{2,3,1,0:T(8,128)(2,1)S(1)} %convert_bitcast_fusion.1) | data formatting | bytes 2097152 | tf_op jit(solution)/shard_map/convert_element_type | solution.py:287
  30.2 7.0 %reshape.103.w_skip = bf16[256,2048]{1,0:T(8,128)(2,1)} reshape(bf16[8,32,64,32]{3,2,1,0:T(8,128)(2,1)} %copy.54) | data formatting | bytes 2097152 | tf_op jit(solution)/shard_map/reshape | solution.py:288
  37.2 2.3 %reshape.105.w_up = bf16[256,1728]{1,0:T(8,128)(2,1)} reshape(bf16[8,32,27,64]{3,2,1,0:T(8,128)(2,1)S(1)} %copy-done) | data formatting | bytes 1769472 | tf_op jit(solution)/shard_map/reshape | solution.py:288
  39.5 0.3 copy.57
  39.8 0.9 copy.61.w_adj
  40.9 0.7 copy.62.w_back
  41.6 0.7 add_convert_fusion.edge
  42.3 46.7 %shard_map.174 = (f32[8,64,256]{2,1,0:T(8,128)}, f32[4,32]{1,0:T(4,128)}, f32[3,3,96,32]{3,2,1,0:T(8,128)}, f32[3,3,3,64,32]{4,3,2,1,0:T(8,128)}, f32[3,288,64]{2,1,0:T(8,128)}) custom-call(s32[2]{0:T(128)} %add_convert_fusion.edge, bf16[6,72,256]{2,1,0:T(8,128)(2,1)} %collective-permute-done.before, bf16[8,72,256]{2,1,0:T(8,128)(2,1)} %pad.7.inflow, ...), custom_call_target="tpu_custom_call" | custom-call | tf_op jit(solution)/shard_map/pallas_call | solution.py:305
  89.0 0.8 reshape.111
  89.8 1.1 reshape.110
  90.9 1.4 reshape.109
  92.3 1.2 reshape.108
  93.5 0.9 maximum_bitcast_fusion
  94.4 0.1 reshape.107
  94.6 0.9 copy.77
  95.4 93.7 %all-reduce.4.cloned.1.call-done = f32[1081,128]{1,0:T(8,128)} async-done(((f32[1081,128]{1,0:T(8,128)}), f32[1081,128]{1,0:T(8,128)}) %all-reduce.4.cloned.1.call-update) | async-done | bytes 553488 | tf_op jit(solution)/shard_map/psum | solution.py:336
  189.1 0.7 slice_reduce_fusion
  189.8 0.7 reshape.113
  190.5 0.9 slice.47
  191.4 0.2 reshape.115
  191.5 0.2 copy.65
  191.7 1.1 fusion.7
  192.8 0.2 reshape.114
  193.0 0.3 copy.64
  193.3 0.1 reshape.116
  193.5 0.8 copy.66
  194.2 0.9 maximum_bitcast_fusion.1
  (34 shorter events, 0.7 us)
Async XLA Ops:
  7.2 181.9 %all-reduce.4.cloned.1.call-start = ((), (), s32[]{:S(2)}) async-start(), calls=%async_computation | async-start | bytes 1114112 | tf_op jit(solution)/shard_map/psum | solution.py:336
  8.4 9.4 %copy-start.7 = (bf16[3,3,3,32,4]{3,4,2,1,0:T(4,128)(2,1)S(1)}, bf16[3,3,3,32,4]{3,4,2,1,0:T(4,128)(2,1)}, u32[]{:S(2)}) copy-start(bf16[3,3,3,32,4]{3,4,2,1,0:T(4,128)(2,1)} %param.18) | copy-start | bytes 20740
  8.4 9.5 %copy-start.1 = (bf16[3,3,3,32,96]{4,3,2,1,0:T(8,128)(2,1)S(1)}, bf16[3,3,3,32,96]{4,3,2,1,0:T(8,128)(2,1)}, u32[]{:S(2)}) copy-start(bf16[3,3,3,32,96]{4,3,2,1,0:T(8,128)(2,1)} %param.20) | copy-start | bytes 497668
  9.7 8.8 %copy-start.5 = (bf16[8,27,27,1]{1,2,3,0:T(8,128)(2,1)S(1)}, bf16[8,27,27,1]{1,2,3,0:T(8,128)(2,1)}, u32[]{:S(2)}) copy-start(bf16[8,27,27,1]{1,2,3,0:T(8,128)(2,1)} %constant.45) | copy-start | bytes 34996
  10.6 31.7 %collective-permute-start = (bf16[6,72,256]{2,1,0:T(8,128)(2,1)}, bf16[6,72,256]{2,1,0:T(8,128)(2,1)}, u32[]{:S(2)}, u32[]{:S(2)}) collective-permute-start(bf16[6,72,256]{2,1,0:T(8,128)(2,1)} %pad_maximum_fusion), channel_id=1, source_target_pairs={{0,1},{1,2},{2,3},{3,4},{4,5},{5,6},{6,7},{7,8},{8,9},{9,10},{10,1... | collective-permute-start | bytes 663560 | tf_op jit(solution)/shard_map/ppermute | solution.py:279
  14.3 27.9 %collective-permute-start.1 = (bf16[6,72,256]{2,1,0:T(8,128)(2,1)}, bf16[6,72,256]{2,1,0:T(8,128)(2,1)}, u32[]{:S(2)}, u32[]{:S(2)}) collective-permute-start(bf16[6,72,256]{2,1,0:T(8,128)(2,1)} %pad_maximum_fusion.1), channel_id=1, source_target_pairs={{1,0},{2,1},{3,2},{4,3},{5,4},{6,5},{7,6},{8,7},{9,8},{10,9},{11,1... | collective-permute-start | bytes 663560 | tf_op jit(solution)/shard_map/ppermute | solution.py:280
  16.4 4.1 %copy-start.8 = (bf16[27,64,1]{1,0,2:T(8,128)(2,1)S(1)}, bf16[27,64,1]{1,0,2:T(8,128)(2,1)}, u32[]{:S(2)}) copy-start(bf16[27,64,1]{1,0,2:T(8,128)(2,1)} %constant.46) | copy-start | bytes 10372
  17.9 3.0 %copy-start.6 = (bf16[8,27,64,1]{2,1,3,0:T(8,128)(2,1)S(1)}, bf16[8,27,64,1]{2,1,3,0:T(8,128)(2,1)}, u32[]{:S(2)}) copy-start(bf16[8,27,64,1]{2,1,3,0:T(8,128)(2,1)} %constant.43) | copy-start | bytes 82948
  18.1 3.0 %copy-start.4 = (bf16[8,27,64,1]{2,1,3,0:T(8,128)(2,1)S(1)}, bf16[8,27,64,1]{2,1,3,0:T(8,128)(2,1)}, u32[]{:S(2)}) copy-start(bf16[8,27,64,1]{2,1,3,0:T(8,128)(2,1)} %constant.44) | copy-start | bytes 82948
  20.5 1.3 copy-start.9
  20.6 1.3 copy-start.10
  30.2 7.0 %copy-start = (bf16[8,32,27,64]{3,2,1,0:T(8,128)(2,1)S(1)}, bf16[8,32,27,64]{3,2,1,0:T(8,128)(2,1)}, u32[]{:S(2)}) copy-start(bf16[8,32,27,64]{3,2,1,0:T(8,128)(2,1)} %convert_bitcast_fusion) | copy-start | bytes 2654212
  40.8 1.4 copy-start.3
  89.0 5.4 %copy-start.2 = (f32[8,64,256]{2,1,0:T(8,128)S(1)}, f32[8,64,256]{2,1,0:T(8,128)}, u32[]{:S(2)}) copy-start(f32[8,64,256]{2,1,0:T(8,128)} %get-tuple-element.9) | copy-start | bytes 1572868
Sparse Core Ops, SparseCore 0:
  94.5 94.5 all-reduce.3

commit v2 on v1

--- a/solution.py
+++ b/solution.py
@@ -17,17 +17,11 @@
 
 def place_tables():
     fine = np.zeros((2, 3, 4), np.float32)
-    coarse = np.zeros((2, 3, 3), np.float32)
-    child = np.zeros((3, 4), np.float32)
     for p in range(2):
         for a in range(3):
             fine[p, a, p + a] = 1
-            coarse[p, a, (p + a - 1) // 2 + 1] = 1
-            child[a, p + 2 - a] += 1
     t_in = np.einsum("pax,qby,rez->pqrabexzy", fine, fine, fine).reshape(8, 27, 64)
-    t_skip = np.einsum("pax,qby,rez->pqrabeyxz", fine, fine, fine).reshape(8, 27, 64)
-    t_up = np.einsum("pax,qby,rez->pqrabeyxz", coarse, coarse, coarse).reshape(8, 27, 27)
-    t_adj = np.einsum("ax,by,ez->abeyxz", child, child, child).reshape(27, 64)
+    t_in = np.einsum("PkD,cd->PkcDd", t_in, np.eye(4, dtype=np.float32)).reshape(8, 108, 256)
     order = np.zeros((8, 8), np.float32)
     for i, (px, py, pz) in enumerate(PARITIES):
         order[i, px * 4 + pz * 2 + py] = 1
@@ -39,7 +33,13 @@
                 split[2 * z - 1 + w, w * LANES + z] = 1
         for p in range(2):
             merge[p * LANES + z, 2 * z + p] = 1
-    return t_in, t_skip, t_up, t_adj, order, split, merge
+    take = np.zeros((80, 64), np.float32)
+    give = np.zeros((64, 64), np.float32)
+    for y in range(16):
+        for c in range(4):
+            take[4 + y * 4 + c, c * 16 + y] = 1
+            give[c * 16 + y, y * 4 + c] = 1
+    return t_in, order, split, merge, take, give
 
 
 def dot(a, b):
@@ -75,11 +75,13 @@
 
 
 def body(
-    edge, before, inflow, after, gp, bias, w_in, w_mid, w_skip, w_up, w_adj, w_back, w_pred,
-    split, merge,
-    pred, g_out, g_skip, g_up, g_mid,
+    edge, before, inflow, after, gp, bias, in_taps, w_mid, skip_taps, up_taps, adj_taps,
+    w_back, w_pred, t_in, split, merge, take, give,
+    pred, packed,
     patch, gpatch, enc_s, pool_s, coarse_s, pre_s, gd_s, gt_s, gct_s, acc_s,
+    w_in, w_skip, w_up, w_adj, out_s, pack_s, mid_s, skip_s,
 ):
+    build_kernels(in_taps, skip_taps, up_taps, adj_taps, t_in, w_in, w_skip, w_up, w_adj)
     first, last = edge[0] == 1, edge[1] == 1
     for ref in (enc_s, gd_s):
         ref[:, :, 0:LANES] = jnp.zeros(ref.shape[:2] + (LANES,), BF16)
@@ -89,7 +91,11 @@
         ref[:, LANES + CELLS :] = jnp.zeros((ref.shape[0], LANES), BF16)
     coarse_s[0:192, :] = jnp.zeros((192, WIDE), BF16)
     coarse_s[7 * 192 : 8 * 192, :] = jnp.zeros((192, WIDE), BF16)
-    g_out[...] = jnp.zeros(g_out.shape, F32)
+    out_s[...] = jnp.zeros(out_s.shape, F32)
+
+    def fine_line(ref, i):
+        rows = jnp.concatenate([ref[c, i] for c in range(4)], axis=0)
+        return dot(take[...], rows).astype(BF16)
 
     def put_inflow(line, value):
         parts = dot(value, split[...])
@@ -98,23 +104,23 @@
 
     def put_gp(line, value):
         parts = dot(value, split[:, LANES : 3 * LANES])
-        block = [rows_to_lanes(parts, 0, 8, w * LANES) for w in range(2)]
+        block = [rows_to_lanes(parts, 4, 8, w * LANES) for w in range(2)]
         gpatch[row(line, 16, 16), :] = jnp.concatenate(block, axis=0).astype(BF16)
 
     def edges(i, c):
-        put_inflow(i, before[i])
-        put_inflow(i + 13, after[i])
+        put_inflow(i, fine_line(before, i))
+        put_inflow(i + 13, fine_line(after, i))
         return c
 
     def middle(i, c):
-        put_inflow(i + 5, inflow[i])
-        put_gp(i + 1, gp[i][4:68])
+        put_inflow(i + 5, fine_line(inflow, i))
+        put_gp(i + 1, fine_line(gp, i))
         return c
 
     lax.fori_loop(0, 5, edges, 0)
     lax.fori_loop(0, 8, middle, 0)
-    put_gp(0, before[5][4:68])
-    put_gp(9, after[5][4:68])
+    put_gp(0, fine_line(before, 5))
+    put_gp(9, fine_line(after, 5))
 
     def encode(xe, c):
         outside = (first & (xe < 2)) | (last & (xe > 5))
@@ -186,11 +192,15 @@
             line = jnp.concatenate(halves, axis=1)
             high = line.astype(BF16)
             low = (line - high.astype(F32)).astype(BF16)
-            pred[2 * xc + px] = dot(high, merge[...]) + dot(low, merge[...])
+            high = dot(give[...], high).astype(BF16)
+            low = dot(give[...], low).astype(BF16)
+            line = dot(high, merge[...]) + dot(low, merge[...])
+            for o in range(4):
+                pred[o, 2 * xc + px] = line[o * 16 : o * 16 + 16]
         full = lax.dot_general(cot, dec, (((1,), (1,)), ((), ())), preferred_element_type=F32)
         for i, (px, py, pz) in enumerate(PARITIES):
             at = (px * 4 + pz * 2 + py) * 4
-            g_out[...] += full[at : at + 4, i * 32 : i * 32 + 32]
+            out_s[0:4, 0:32] += full[at : at + 4, i * 32 : i * 32 + 32]
         put_grad(xc, (0, 1), grad)
         gt_s[row(xc, CELLS, CELLS), :] = grad.T.astype(BF16)
         return c
@@ -230,7 +240,7 @@
                 pool_s[(xc + 1) * 96 : (xc + 1) * 96 + 288, dy * LANES : dy * LANES + CELLS],
                 gct_s[xc * CELLS : (xc + 1) * CELLS, :],
             )
-        g_mid[dy] = total
+        mid_s[dy] = total
     for yw, (par, start) in enumerate(WINDOW):
         total = jnp.zeros((512, 256), F32)
         for xc in range(4):
@@ -245,7 +255,7 @@
             for i, (px, py, pz) in enumerate(PARITIES):
                 at = (py + b) * 512 + (px + a) * 128 + pz * 32
                 total = total + acc_s[at : at + 96, i * 32 : i * 32 + 32]
-            g_skip[a, b] = total
+            skip_s[a * 3 + b] = total
     for dy in range(3):
         total = jnp.zeros((576, 256), F32)
         for xc in range(4):
@@ -254,65 +264,177 @@
                 gt_s[xc * CELLS : (xc + 1) * CELLS, :],
             )
         acc_s[dy * 576 : dy * 576 + 576, :] = total
+    zero = jnp.zeros((128, 32), F32)
     for a in range(3):
         for b in range(3):
+            taps = []
+            mid = mid_s[b, a * 96 : a * 96 + 96, :]
             for e in range(3):
                 total = jnp.zeros((64, 32), F32)
                 for i, (px, py, pz) in enumerate(PARITIES):
                     dx, dy, dz = (px + a + 1) // 2, (py + b + 1) // 2, (pz + e + 1) // 2
                     at = dy * 576 + dx * 192 + dz * 64
                     total = total + acc_s[at : at + 64, i * 32 : i * 32 + 32]
-                g_up[a, b, e] = total
+                own = slice(e * 32, e * 32 + 32)
+                taps.append(jnp.concatenate([total, skip_s[a * 3 + b, own], mid[own, 0:32]], axis=0))
+            main = jnp.concatenate(taps + [zero], axis=1).T
+            rest = jnp.concatenate([mid[:, 32:64], zero[0:32]], axis=0)
+            rest = jnp.concatenate([rest, zero, zero, zero], axis=1).T
+            for e in range(3):
+                at = ((a * 3 + b) * 3 + e) * 40
+                pack_s[at : at + 32, :] = main[e * 32 : e * 32 + 32]
+                own = slice(e * 32, e * 32 + 32)
+                pack_s[at + 32 : at + 40, :] = jnp.concatenate(
+                    [rest[g * 8 : g * 8 + 8, own] for g in range(4)], axis=1
+                )
+    pack_s[1080:1088, :] = out_s[...]
+    if pack_s.shape[0] > 1088:
+        pack_s[1088:, :] = jnp.zeros((pack_s.shape[0] - 1088, 128), F32)
+    packed[...] = pack_s[...].astype(packed.dtype)
+
+
+def build_kernels(in_taps, skip_taps, up_taps, adj_taps, t_in, w_in, w_skip, w_up, w_adj):
+    gap = jnp.zeros((32, 64), F32)
+    w_skip[...] = jnp.zeros(w_skip.shape, BF16)
+    for i, (px, py, pz) in enumerate(PARITIES):
+        rows = slice(i * 32, i * 32 + 32)
+        w_in[rows, :] = dot(in_taps[...], t_in[i]).astype(BF16)
+        for a in range(3):
+            for b in range(3):
+                v = skip_taps[a * 3 + b].astype(F32)
+                v = jnp.concatenate([gap[:, 0:32], v] if pz else [v, gap[:, 0:32]], axis=1)
+                at = (py + b) * 512 + (px + a) * 128
+                w_skip[rows, at : at + 128] = v.astype(BF16)
+        pieces = []
+        for dy in range(3):
+            for dx in range(3):
+                v = jnp.zeros((32, 192), F32)
+                for a in range(3):
+                    for b in range(3):
+                        if (px + a + 1) // 2 == dx and (py + b + 1) // 2 == dy:
+                            v = v + up_taps[a * 3 + b].astype(F32)
+                e0, e1, e2 = v[:, 0:64], v[:, 64:128], v[:, 128:192]
+                pieces += [gap, e0 + e1, e2] if pz else [e0, e1 + e2, gap]
+        w_up[rows, :] = jnp.concatenate(pieces, axis=1).astype(BF16)
+    zero = jnp.zeros((64, 32), F32)
+    along_z = []
+    for k in range(9):
+        v = adj_taps[k].astype(F32)
+        along_z.append(jnp.concatenate([v, zero], axis=1) + jnp.concatenate([zero, v], axis=1))
+    reach = ((2,), (1, 2), (0, 1), (0,))
+    for yw in range(4):
+        for xw in range(4):
+            v = jnp.zeros((64, 128), F32)
+            for b in reach[yw]:
+                for a in reach[xw]:
+                    v = v + along_z[a * 3 + b]
+            at = yw * 512 + xw * 128
+            w_adj[:, at : at + 128] = v.astype(BF16)
+
+
+def sum_body(n, packed, g_dec, g_mid, g_out, got, total_s, whole, flat, send1, recv1, send2, recv2):
+    me = lax.axis_index("block")
+    chunk = packed.shape[0] // n
+    barrier = pltpu.get_barrier_semaphore()
+
+    def greet(k, c):
+        pl.semaphore_signal(
+            barrier, 1, device_id={"block": lax.rem(me + k, n)},
+            device_id_type=pl.DeviceIdType.MESH,
+        )
+        return c
+
+    lax.fori_loop(1, n, greet, 0)
+    pl.semaphore_wait(barrier, n - 1)
+
+    def scatter(k):
+        to = lax.rem(me + k, n)
+        return pltpu.make_async_remote_copy(
+            src_ref=packed.at[pl.ds(pl.multiple_of(to * chunk, 16), chunk)],
+            dst_ref=got.at[k],
+            send_sem=send1.at[k],
+            recv_sem=recv1.at[k],
+            device_id={"block": to},
+            device_id_type=pl.DeviceIdType.MESH,
+        )
+
+    def gather(k):
+        return pltpu.make_async_remote_copy(
+            src_ref=total_s,
+            dst_ref=whole.at[k],
+            send_sem=send2.at[k],
+            recv_sem=recv2.at[k],
+            device_id={"block": lax.rem(me + k, n)},
+            device_id_type=pl.DeviceIdType.MESH,
+        )
+
+    def each(f):
+        lax.fori_loop(1, n, lambda k, c: (f(k), c)[1], 0)
+
+    each(lambda k: scatter(k).start())
+
+    def add(k, total):
+        scatter(k).wait_recv()
+        return total + got[k].astype(F32)
+
+    own = packed[pl.ds(pl.multiple_of(me * chunk, 16), chunk), :].astype(F32)
+    total = lax.fori_loop(1, n, add, own).astype(BF16)
+    total_s[...] = total
+    each(lambda k: gather(k).start())
+    flat[pl.ds(pl.multiple_of(me * chunk, 16), chunk), :] = total.astype(F32)
+
+    def place(k, c):
+        gather(k).wait_recv()
+        at = lax.rem(me - k + n, n) * chunk
+        flat[pl.ds(pl.multiple_of(at, 16), chunk), :] = whole[k].astype(F32)
+        return c
+
+    lax.fori_loop(1, n, place, 0)
+    each(lambda k: scatter(k).wait_send())
+    each(lambda k: gather(k).wait_send())
+
+    def unpack(k, c):
+        main = flat[pl.ds(pl.multiple_of(k * 40, 8), 32), :]
+        rest = flat[pl.ds(pl.multiple_of(k * 40 + 32, 8), 8), :]
+        g_dec[k] = main[:, 0:96]
+        g_mid[k] = jnp.concatenate(
+            [main[:, 96:128]] + [rest[:, g * 32 : g * 32 + 32] for g in range(4)], axis=0
+        )
+        return c
+
+    lax.fori_loop(0, 27, unpack, 0)
+    g_out[...] = flat[1080:1084, 0:32]
 
 
 def shards(inflow, speed_bin, bin_table, w_in, w_mid, w_dec, w_out, grad_pred):
-    t_in, t_skip, t_up, t_adj, order, split, merge = (
-        jnp.asarray(t, BF16) for t in place_tables()
-    )
-    lines = lambda f: jnp.pad(
-        f.transpose(1, 2, 0, 3).reshape(f.shape[1], 64, 256), ((0, 0), (4, 4), (0, 0))
-    )
-    field, cot = lines(inflow), lines(grad_pred)
+    t_in, order, split, merge, take, give = (jnp.asarray(t, BF16) for t in place_tables())
     devices = lax.axis_size("block")
     up = [(i, i + 1) for i in range(devices - 1)]
     down = [(i + 1, i) for i in range(devices - 1)]
-    before = lax.ppermute(jnp.concatenate([field[3:8], cot[7:8]], axis=0), "block", up)
-    after = lax.ppermute(jnp.concatenate([field[0:5], cot[0:1]], axis=0), "block", down)
+    ends = jnp.concatenate([inflow[:, 3:8], grad_pred[:, 7:8]], axis=1)
+    starts = jnp.concatenate([inflow[:, 0:5], grad_pred[:, 0:1]], axis=1)
+    before = lax.ppermute(ends, "block", up)
+    after = lax.ppermute(starts, "block", down)
     me = lax.axis_index("block")
     edge = jnp.stack([me == 0, me == devices - 1]).astype(jnp.int32)
     bias = jnp.tile(lax.dynamic_index_in_dim(bin_table, speed_bin[0], 0, False), 8)
     bias = bias.astype(F32)[:, None]
-    spread = lambda t, w: (
-        jnp.einsum("PkD,koc->PoDc", t, w.reshape((27,) + w.shape[3:]), preferred_element_type=F32)
-        .astype(BF16)
-        .reshape(256, -1)
-    )
-    k_in = spread(t_in, w_in)
-    k_skip = spread(t_skip, w_dec[..., 64:])
-    k_up = spread(t_up, w_dec[..., :64])
+    w_up, w_skip = w_dec[..., :64], w_dec[..., 64:]
+    in_taps = w_in.transpose(3, 0, 1, 2, 4).reshape(32, 108)
+    skip_taps = w_skip.transpose(0, 1, 3, 2, 4).reshape(9, 32, 96)
+    up_taps = w_up.transpose(0, 1, 3, 2, 4).reshape(9, 32, 192)
+    adj_taps = w_up[:, :, ::-1].transpose(0, 1, 4, 2, 3).reshape(9, 64, 96)
     k_mid = w_mid.transpose(3, 1, 0, 2, 4).reshape(64, 864)
-    k_adj = (
-        jnp.einsum(
-            "kD,koc->cDo", t_adj, w_dec[..., :64].reshape(27, 32, 64), preferred_element_type=F32
-        )
-        .astype(BF16)
-        .reshape(64, 2048)
-    )
+    chunk = -(-1088 // (16 * devices)) * 16
     k_back = (order[:, None, :, None] * w_out.T[None, :, None, :]).reshape(256, 32)
     k_pred = k_back.T
     vmem = pl.BlockSpec(memory_space=pltpu.VMEM)
     shape = jax.ShapeDtypeStruct
-    pred, g_out, g_skip, g_up, g_mid = pl.pallas_call(
+    pred, packed = pl.pallas_call(
         body,
-        out_shape=(
-            shape((8, 64, 256), F32),
-            shape((4, 32), F32),
-            shape((3, 3, 96, 32), F32),
-            shape((3, 3, 3, 64, 32), F32),
-            shape((3, 288, 64), F32),
-        ),
-        in_specs=[pl.BlockSpec(memory_space=pltpu.SMEM)] + [vmem] * 14,
-        out_specs=[vmem] * 5,
+        out_shape=(shape((4, 8, 16, 256), F32), shape((chunk * devices, 128), BF16)),
+        in_specs=[pl.BlockSpec(memory_space=pltpu.SMEM)] + [vmem] * 17,
+        out_specs=[vmem] * 2,
         scratch_shapes=[
             pltpu.VMEM((18 * 64, CELLS), BF16),
             pltpu.VMEM((10 * 16, CELLS), BF16),
@@ -324,26 +446,37 @@
             pltpu.VMEM((4 * CELLS, 256), BF16),
             pltpu.VMEM((4 * CELLS, 64), BF16),
             pltpu.VMEM((2048, 256), F32),
+            pltpu.VMEM((256, 256), BF16),
+            pltpu.VMEM((256, 2048), BF16),
+            pltpu.VMEM((256, 1728), BF16),
+            pltpu.VMEM((64, 2048), BF16),
+            pltpu.VMEM((8, 128), F32),
+            pltpu.VMEM((chunk * devices, 128), F32),
+            pltpu.VMEM((3, 288, 64), F32),
+            pltpu.VMEM((9, 96, 32), F32),
         ],
         compiler_params=pltpu.CompilerParams(vmem_limit_bytes=56 * 1024 * 1024),
     )(
-        edge, before, field, after, cot, bias, k_in, k_mid, k_skip, k_up, k_adj, k_back, k_pred,
-        split, merge,
+        edge, before, inflow, after, grad_pred, bias, in_taps, k_mid, skip_taps, up_taps, adj_taps,
+        k_back, k_pred, t_in, split, merge, take, give,
     )
-    flat = jnp.concatenate(
-        [g_skip.reshape(-1), g_up.reshape(-1), g_mid.reshape(-1), g_out.reshape(-1)]
-    ).reshape(-1, 128)
-    flat = lax.psum(flat, "block").reshape(-1)
-    ends = np.cumsum([27648, 55296, 55296, 128])
-    s_skip, s_up, s_mid, s_out = (
-        flat[e - n : e] for e, n in zip(ends, (27648, 55296, 55296, 128))
-    )
-    grad_w_dec = jnp.concatenate(
-        [s_up.reshape(3, 3, 3, 64, 32), s_skip.reshape(3, 3, 3, 32, 32)], axis=3
-    ).swapaxes(3, 4)
-    grad_w_mid = s_mid.reshape(3, 3, 3, 32, 64).transpose(1, 0, 2, 4, 3)
-    pred = pred.reshape(8, 16, 4, 256).transpose(2, 0, 1, 3)
-    return (pred, s_out.reshape(4, 32), grad_w_dec, grad_w_mid)
+    g_dec, g_mid, g_out = pl.pallas_call(
+        lambda *refs: sum_body(devices, *refs),
+        out_shape=(shape((27, 32, 96), F32), shape((27, 64, 32), F32), shape((4, 32), F32)),
+        in_specs=[vmem],
+        out_specs=[vmem] * 3,
+        scratch_shapes=[
+            pltpu.VMEM((devices, chunk, 128), BF16),
+            pltpu.VMEM((chunk, 128), BF16),
+            pltpu.VMEM((devices, chunk, 128), BF16),
+            pltpu.VMEM((chunk * devices, 128), F32),
+        ]
+        + [pltpu.SemaphoreType.DMA((devices,))] * 4,
+        compiler_params=pltpu.CompilerParams(
+            collective_id=0, has_side_effects=True, vmem_limit_bytes=32 * 1024 * 1024
+        ),
+    )(packed)
+    return (pred, g_out, g_dec.reshape(3, 3, 3, 32, 96), g_mid.reshape(3, 3, 3, 64, 32))
 
 
 def solution(mesh):

time: 203 us -> 96.9 us (0.48)
  waiting for transfers between devices: 93.7 us -> 0.01 us
  Pallas kernels: 46.7 us -> 77 us
  local copies, waits for them, and re-layouts: 34.5 us -> 12.1 us
  between operations: 14.9 us -> 1.45 us
  matrix products: 3.25 us -> 0 us
  other arithmetic: 4.64 us -> 1.45 us
    psum x1 -> x0, waiting for transfers between devices: 93.7 us -> none  [shards(): flat = lax.psum(flat, 'block').reshape(-1)]
    pallas_call x1 -> x2, Pallas kernels: 46.7 us -> 77 us  [the longest x1 50.7 us: shards(): pl.pallas_call(body, out_shape=(shape((4, 8, 16, 256), F32), shape((chunk...]
    reshape x21 -> x5, local copies, waits for them, and re-layouts: 19.1 us -> 3.18 us  [the longest x1 0.87 us: shards(): up_taps = w_up.transpose(0, 1, 3, 2, 4).reshape(9, 32, 192)]
    convert_element_type x3 -> x0, local copies, waits for them, and re-layouts: 4.32 us -> none  [the longest x2 3.97 us: shards(): spread = lambda t, w: jnp.einsum('PkD,koc->PoDc', t, w.reshape((27,) + w....]
    unnamed x23 -> x21, local copies, waits for them, and re-layouts: 0.85 us -> 4.14 us
    dot_general x4 -> x0, matrix products: 3.25 us -> none  [the longest x3 2.92 us: shards(): jnp.einsum('PkD,koc->PoDc', t, w.reshape((27,) + w.shape[3:]), preferred_...]
  transfers between devices with their start and end apart: 3 -> 2, of which waited for: 1 -> 0; matrix products, arithmetic and copies ran while one was open for 14% -> 8% of each run, Pallas kernels for 0% -> 0%
where the time goes in v2:
time: 96.9 us; the launch traced here: 95.8 us
  Pallas kernels  77 us (79%)
  local copies, waits for them, and re-layouts  12.1 us (12%)
  starting transfers between devices  3.79 us (4%)
  other arithmetic  1.45 us (1%)
  between operations  1.45 us (1%)
    pallas_call x1, Pallas kernels, shards(): pl.pallas_call(body, out_shape=(shape((4, 8, 16, 256), F32), shape((chunk...  50.7 us
    pallas_call x1, Pallas kernels, shards(): pl.pallas_call(lambda *refs: sum_body(devices, *refs), out_shape=(shape((...  26.3 us
    unnamed x21, local copies, waits for them, and re-layouts  4.14 us
    ppermute x1, starting transfers between devices, shards(): before = lax.ppermute(ends, 'block', up)  2.5 us
  transfers between devices with their start and end apart: 2, of which 0 were waited for; matrix products, arithmetic and copies ran while one was open for 8% of the time, Pallas kernels for 0%

profile of v2, /device:TPU:0, one launch (start us, length us, event | category | flops | bytes accessed | tf_op | source)
XLA Modules:
  0.0 95.8 jit_solution(10442721321384798661)
XLA Ops:
  0.6 0.8 fusion.1
  1.4 1.0 %fusion = (bf16[4,5,16,256]{3,2,1,0:T(8,128)(2,1)S(1)}, bf16[4,5,16,256]{3,2,1,0:T(8,128)(2,1)S(1)}) fusion(bf16[4,8,16,256]{3,2,1,0:T(8,128)(2,1)} %inflow.1), kind=kLoop, calls=%fused_computation.7 | loop fusion | bytes 655360 | tf_op jit(solution)/shard_map/slice | solution.py:415
  2.5 0.0 copy-start.1
  2.5 2.5 %collective-permute-start = (bf16[4,6,16,256]{3,2,1,0:T(8,128)(2,1)S(1)}, bf16[4,6,16,256]{3,2,1,0:T(8,128)(2,1)S(1)}, u32[]{:S(2)}, u32[]{:S(2)}) collective-permute-start(bf16[4,6,16,256]{3,2,1,0:T(8,128)(2,1)S(1)} %pad_maximum_fusion), channel_id=1, source_target_pairs={{0,1},{1,2},{2,3},{3,4},{4,5},{5,6},{6,7},{7,8},{8,9},{9,10},{10,1... | collective-permute-start | bytes 589832 | tf_op jit(solution)/shard_map/ppermute | solution.py:416
  5.0 1.3 %collective-permute-start.1 = (bf16[4,6,16,256]{3,2,1,0:T(8,128)(2,1)S(1)}, bf16[4,6,16,256]{3,2,1,0:T(8,128)(2,1)S(1)}, u32[]{:S(2)}, u32[]{:S(2)}) collective-permute-start(bf16[4,6,16,256]{3,2,1,0:T(8,128)(2,1)S(1)} %pad_maximum_fusion.1), channel_id=1, source_target_pairs={{1,0},{2,1},{3,2},{4,3},{5,4},{6,5},{7,6},{8,7},{9,8},{10,9},{11,1... | collective-permute-start | bytes 589832 | tf_op jit(solution)/shard_map/ppermute | solution.py:417
  6.3 0.0 copy-done.1
  6.3 0.1 slice_bitcast_fusion
  6.5 0.0 copy-start.6
  6.5 0.1 fusion.2
  7.2 0.0 copy-done.6
  7.2 0.0 copy-start.7
  7.2 0.0 copy-start.8
  7.3 0.0 copy-start.2
  7.3 0.7 copy.29.in_taps
  8.0 0.0 copy-done.7
  8.0 0.0 copy-done.8
  8.0 0.1 broadcast_multiply_fusion
  8.0 0.1 mul.20
  8.1 0.0 copy-start.5
  8.2 0.7 copy.32.w_back
  8.9 0.0 copy-done.5
  8.9 0.7 bitcast_convert_fusion
  9.6 0.8 convert_element_type.25.bias
  10.4 0.0 copy-done.2
  10.4 0.8 copy.30.w_mid
  11.2 0.2 copy.26
  11.3 0.8 reshape.50.skip_taps
  12.1 0.8 copy.31.adj_taps
  12.9 0.2 copy.27
  13.1 0.9 reshape.51.up_taps
  14.0 0.6 add_convert_fusion.edge
  14.6 0.0 collective-permute-done.before
  14.6 0.0 copy-start.3
  14.6 0.0 collective-permute-done.1.after
  14.6 0.0 copy-start.4
  14.6 0.7 copy-done.3
  15.3 0.1 copy-done.4
  15.4 50.7 %shard_map.165 = (f32[4,8,16,256]{3,2,1,0:T(8,128)}, bf16[1280,128]{1,0:T(8,128)(2,1)}) custom-call(s32[2]{0:T(128)} %add_convert_fusion.edge, bf16[4,6,16,256]{3,2,1,0:T(8,128)(2,1)} %copy-done.3, bf16[4,8,16,256]{3,2,1,0:T(8,128)(2,1)} %inflow.1, bf16[4,6,16,256]{3,2,1,0:T(8,128)(2,1)} %copy-done.4, bf16[4,8,16,256]{3,2,1,0:T(8,128)(2,1)} %gp.1, ...), custom_call_target="tpu_custom_call" | custom-call | tf_op jit(solution)/shard_map/pallas_call | solution.py:433
  66.1 0.0 copy-start
  66.1 1.0 %copy-done = bf16[1280,128]{1,0:T(8,128)(2,1)S(1)} copy-done((bf16[1280,128]{1,0:T(8,128)(2,1)S(1)}, bf16[1280,128]{1,0:T(8,128)(2,1)}, u32[]{:S(2)}) %copy-start) | copy-done | bytes 327704
  67.0 26.3 %shard_map.166 = (f32[27,32,96]{2,1,0:T(8,128)S(1)}, f32[27,64,32]{2,1,0:T(8,128)S(1)}, f32[4,32]{1,0:T(4,128)S(1)}) custom-call(bf16[1280,128]{1,0:T(8,128)(2,1)S(1)} %copy-done), custom_call_target="tpu_custom_call" | custom-call | tf_op jit(solution)/shard_map/pallas_call | solution.py:463
  93.4 1.1 %copy.33 = f32[3,3,3,64,32]{3,4,2,1,0:T(8,128)} copy(f32[3,3,3,64,32]{4,3,2,1,0:T(8,128)S(1)} %bitcast.29) | data formatting | bytes 442368
  94.4 0.6 copy.37
  95.0 0.8 copy.38
  (6 shorter events, 0.1 us)
Async XLA Ops:
  2.5 3.9 %copy-start.1 = (bf16[3,3,3,32,96]{4,3,2,1,0:T(8,128)(2,1)S(1)}, bf16[3,3,3,32,96]{4,3,2,1,0:T(8,128)(2,1)}, u32[]{:S(2)}) copy-start(bf16[3,3,3,32,96]{4,3,2,1,0:T(8,128)(2,1)} %param.19) | copy-start | bytes 497668
  2.5 12.1 %collective-permute-start = (bf16[4,6,16,256]{3,2,1,0:T(8,128)(2,1)S(1)}, bf16[4,6,16,256]{3,2,1,0:T(8,128)(2,1)S(1)}, u32[]{:S(2)}, u32[]{:S(2)}) collective-permute-start(bf16[4,6,16,256]{3,2,1,0:T(8,128)(2,1)S(1)} %pad_maximum_fusion), channel_id=1, source_target_pairs={{0,1},{1,2},{2,3},{3,4},{4,5},{5,6},{6,7},{7,8},{8,9},{9,10},{10,1... | collective-permute-start | bytes 589832 | tf_op jit(solution)/shard_map/ppermute | solution.py:416
  5.0 9.6 %collective-permute-start.1 = (bf16[4,6,16,256]{3,2,1,0:T(8,128)(2,1)S(1)}, bf16[4,6,16,256]{3,2,1,0:T(8,128)(2,1)S(1)}, u32[]{:S(2)}, u32[]{:S(2)}) collective-permute-start(bf16[4,6,16,256]{3,2,1,0:T(8,128)(2,1)S(1)} %pad_maximum_fusion.1), channel_id=1, source_target_pairs={{1,0},{2,1},{3,2},{4,3},{5,4},{6,5},{7,6},{8,7},{9,8},{10,9},{11,1... | collective-permute-start | bytes 589832 | tf_op jit(solution)/shard_map/ppermute | solution.py:417
  6.5 0.7 copy-start.6
  7.2 0.7 copy-start.7
  7.2 0.7 copy-start.8
  7.3 3.1 %copy-start.2 = (bf16[3,3,3,64,32]{3,4,2,1,0:T(8,128)(2,1)S(1)}, bf16[3,3,3,64,32]{3,4,2,1,0:T(8,128)(2,1)}, u32[]{:S(2)}) copy-start(bf16[3,3,3,64,32]{3,4,2,1,0:T(8,128)(2,1)} %param.18) | copy-start | bytes 331780
  8.1 0.7 copy-start.5
  14.6 0.7 copy-start.3
  14.6 0.7 copy-start.4
  66.1 1.0 %copy-start = (bf16[1280,128]{1,0:T(8,128)(2,1)S(1)}, bf16[1280,128]{1,0:T(8,128)(2,1)}, u32[]{:S(2)}) copy-start(bf16[1280,128]{1,0:T(8,128)(2,1)} %get-tuple-element.10.refs_0_) | copy-start | bytes 983044

commit v3 on v2

--- a/solution.py
+++ b/solution.py
@@ -42,6 +42,10 @@
     return t_in, order, split, merge, take, give
 
 
+def sigmoid(v):
+    return 0.5 * jnp.tanh(0.5 * v) + 0.5
+
+
 def dot(a, b):
     return jnp.dot(a, b, preferred_element_type=F32)
 
@@ -147,7 +151,7 @@
             )
         pre_s[xk] = pre
         outside = (first & (xk < 1)) | (last & (xk > 4))
-        put_coarse(coarse_s, xk + 1, jnp.where(outside, 0.0, pre * jax.nn.sigmoid(pre)))
+        put_coarse(coarse_s, xk + 1, jnp.where(outside, 0.0, pre * sigmoid(pre)))
         return c
 
     lax.fori_loop(0, 6, middle_level, 0)
@@ -174,7 +178,7 @@
 
     def decode(xc, c):
         v = decode_pre(xc, (0, 256))
-        sigma = jax.nn.sigmoid(v)
+        sigma = sigmoid(v)
         dec = (v * sigma).astype(BF16)
         cot = gpatch[row(2 * xc + 1, 32, 16), :]
         grad = dot(w_back[...], cot) * (sigma * (1.0 + v * (1.0 - sigma)))
@@ -207,7 +211,7 @@
 
     def rim(xc, px, line):
         v = decode_pre(xc, (px * 128, px * 128 + 128))
-        sigma = jax.nn.sigmoid(v)
+        sigma = sigmoid(v)
         back = dot(
             w_back[px * 128 : px * 128 + 128, px * 16 : px * 16 + 16],
             gpatch[line * 16 : line * 16 + 16, :],
@@ -226,7 +230,7 @@
                 gd_s[par, row(xc, 512, 256), start : start + CELLS],
             )
         pre = pre_s[xc + 1]
-        sigma = jax.nn.sigmoid(pre)
+        sigma = sigmoid(pre)
         v = v * (sigma * (1.0 + pre * (1.0 - sigma)))
         gct_s[row(xc, CELLS, CELLS), :] = v.T.astype(BF16)
         return c

time: 96.9 us -> 97 us (level)
  no operation moved by 1% of the time
where the time goes in v3:
time: 97 us; the launch traced here: 95.9 us
  Pallas kernels  77.1 us (79%)
  local copies, waits for them, and re-layouts  12.1 us (12%)
  starting transfers between devices  3.79 us (4%)
  other arithmetic  1.45 us (1%)
  between operations  1.45 us (1%)
    pallas_call x1, Pallas kernels, shards(): pl.pallas_call(body, out_shape=(shape((4, 8, 16, 256), F32), shape((chunk...  50.8 us
    pallas_call x1, Pallas kernels, shards(): pl.pallas_call(lambda *refs: sum_body(devices, *refs), out_shape=(shape((...  26.4 us
    unnamed x21, local copies, waits for them, and re-layouts  4.14 us
    ppermute x1, starting transfers between devices, shards(): before = lax.ppermute(ends, 'block', up)  2.5 us
  transfers between devices with their start and end apart: 2, of which 0 were waited for; matrix products, arithmetic and copies ran while one was open for 8% of the time, Pallas kernels for 0%

profile of v3, /device:TPU:0, one launch (start us, length us, event | category | flops | bytes accessed | tf_op | source)
XLA Modules:
  0.0 95.9 jit_solution(18027393488796533011)
XLA Ops:
  0.6 0.8 fusion.1
  1.4 1.0 %fusion = (bf16[4,5,16,256]{3,2,1,0:T(8,128)(2,1)S(1)}, bf16[4,5,16,256]{3,2,1,0:T(8,128)(2,1)S(1)}) fusion(bf16[4,8,16,256]{3,2,1,0:T(8,128)(2,1)} %inflow.1), kind=kLoop, calls=%fused_computation.7 | loop fusion | bytes 655360 | tf_op jit(solution)/shard_map/slice | solution.py:419
  2.5 0.0 copy-start.1
  2.5 2.5 %collective-permute-start = (bf16[4,6,16,256]{3,2,1,0:T(8,128)(2,1)S(1)}, bf16[4,6,16,256]{3,2,1,0:T(8,128)(2,1)S(1)}, u32[]{:S(2)}, u32[]{:S(2)}) collective-permute-start(bf16[4,6,16,256]{3,2,1,0:T(8,128)(2,1)S(1)} %pad_maximum_fusion), channel_id=1, source_target_pairs={{0,1},{1,2},{2,3},{3,4},{4,5},{5,6},{6,7},{7,8},{8,9},{9,10},{10,1... | collective-permute-start | bytes 589832 | tf_op jit(solution)/shard_map/ppermute | solution.py:420
  5.0 1.3 %collective-permute-start.1 = (bf16[4,6,16,256]{3,2,1,0:T(8,128)(2,1)S(1)}, bf16[4,6,16,256]{3,2,1,0:T(8,128)(2,1)S(1)}, u32[]{:S(2)}, u32[]{:S(2)}) collective-permute-start(bf16[4,6,16,256]{3,2,1,0:T(8,128)(2,1)S(1)} %pad_maximum_fusion.1), channel_id=1, source_target_pairs={{1,0},{2,1},{3,2},{4,3},{5,4},{6,5},{7,6},{8,7},{9,8},{10,9},{11,1... | collective-permute-start | bytes 589832 | tf_op jit(solution)/shard_map/ppermute | solution.py:421
  6.3 0.0 copy-done.1
  6.3 0.1 slice_bitcast_fusion
  6.5 0.0 copy-start.6
  6.5 0.1 fusion.2
  7.2 0.0 copy-done.6
  7.2 0.0 copy-start.7
  7.2 0.0 copy-start.8
  7.3 0.0 copy-start.2
  7.3 0.7 copy.29.in_taps
  8.0 0.0 copy-done.7
  8.0 0.0 copy-done.8
  8.0 0.1 broadcast_multiply_fusion
  8.0 0.1 mul.20
  8.1 0.0 copy-start.5
  8.2 0.7 copy.32.w_back
  8.9 0.0 copy-done.5
  8.9 0.7 bitcast_convert_fusion
  9.6 0.8 convert_element_type.25.bias
  10.4 0.0 copy-done.2
  10.4 0.8 copy.30.w_mid
  11.2 0.2 copy.26
  11.3 0.8 reshape.50.skip_taps
  12.1 0.8 copy.31.adj_taps
  12.9 0.2 copy.27
  13.1 0.9 reshape.51.up_taps
  14.0 0.6 add_convert_fusion.edge
  14.6 0.0 collective-permute-done.before
  14.6 0.0 copy-start.3
  14.6 0.0 collective-permute-done.1.after
  14.6 0.0 copy-start.4
  14.6 0.7 copy-done.3
  15.3 0.1 copy-done.4
  15.4 50.8 %shard_map.165 = (f32[4,8,16,256]{3,2,1,0:T(8,128)}, bf16[1280,128]{1,0:T(8,128)(2,1)}) custom-call(s32[2]{0:T(128)} %add_convert_fusion.edge, bf16[4,6,16,256]{3,2,1,0:T(8,128)(2,1)} %copy-done.3, bf16[4,8,16,256]{3,2,1,0:T(8,128)(2,1)} %inflow.1, bf16[4,6,16,256]{3,2,1,0:T(8,128)(2,1)} %copy-done.4, bf16[4,8,16,256]{3,2,1,0:T(8,128)(2,1)} %gp.1, ...), custom_call_target="tpu_custom_call" | custom-call | tf_op jit(solution)/shard_map/pallas_call | solution.py:437
  66.1 0.0 copy-start
  66.1 1.0 %copy-done = bf16[1280,128]{1,0:T(8,128)(2,1)S(1)} copy-done((bf16[1280,128]{1,0:T(8,128)(2,1)S(1)}, bf16[1280,128]{1,0:T(8,128)(2,1)}, u32[]{:S(2)}) %copy-start) | copy-done | bytes 327704
  67.1 26.4 %shard_map.166 = (f32[27,32,96]{2,1,0:T(8,128)S(1)}, f32[27,64,32]{2,1,0:T(8,128)S(1)}, f32[4,32]{1,0:T(4,128)S(1)}) custom-call(bf16[1280,128]{1,0:T(8,128)(2,1)S(1)} %copy-done), custom_call_target="tpu_custom_call" | custom-call | tf_op jit(solution)/shard_map/pallas_call | solution.py:467
  93.5 1.1 %copy.33 = f32[3,3,3,64,32]{3,4,2,1,0:T(8,128)} copy(f32[3,3,3,64,32]{4,3,2,1,0:T(8,128)S(1)} %bitcast.29) | data formatting | bytes 442368
  94.5 0.6 copy.37
  95.1 0.8 copy.38
  (6 shorter events, 0.1 us)
Async XLA Ops:
  2.5 3.9 %copy-start.1 = (bf16[3,3,3,32,96]{4,3,2,1,0:T(8,128)(2,1)S(1)}, bf16[3,3,3,32,96]{4,3,2,1,0:T(8,128)(2,1)}, u32[]{:S(2)}) copy-start(bf16[3,3,3,32,96]{4,3,2,1,0:T(8,128)(2,1)} %param.19) | copy-start | bytes 497668
  2.5 12.1 %collective-permute-start = (bf16[4,6,16,256]{3,2,1,0:T(8,128)(2,1)S(1)}, bf16[4,6,16,256]{3,2,1,0:T(8,128)(2,1)S(1)}, u32[]{:S(2)}, u32[]{:S(2)}) collective-permute-start(bf16[4,6,16,256]{3,2,1,0:T(8,128)(2,1)S(1)} %pad_maximum_fusion), channel_id=1, source_target_pairs={{0,1},{1,2},{2,3},{3,4},{4,5},{5,6},{6,7},{7,8},{8,9},{9,10},{10,1... | collective-permute-start | bytes 589832 | tf_op jit(solution)/shard_map/ppermute | solution.py:420
  5.0 9.6 %collective-permute-start.1 = (bf16[4,6,16,256]{3,2,1,0:T(8,128)(2,1)S(1)}, bf16[4,6,16,256]{3,2,1,0:T(8,128)(2,1)S(1)}, u32[]{:S(2)}, u32[]{:S(2)}) collective-permute-start(bf16[4,6,16,256]{3,2,1,0:T(8,128)(2,1)S(1)} %pad_maximum_fusion.1), channel_id=1, source_target_pairs={{1,0},{2,1},{3,2},{4,3},{5,4},{6,5},{7,6},{8,7},{9,8},{10,9},{11,1... | collective-permute-start | bytes 589832 | tf_op jit(solution)/shard_map/ppermute | solution.py:421
  6.5 0.7 copy-start.6
  7.2 0.7 copy-start.7
  7.2 0.7 copy-start.8
  7.3 3.1 %copy-start.2 = (bf16[3,3,3,64,32]{3,4,2,1,0:T(8,128)(2,1)S(1)}, bf16[3,3,3,64,32]{3,4,2,1,0:T(8,128)(2,1)}, u32[]{:S(2)}) copy-start(bf16[3,3,3,64,32]{3,4,2,1,0:T(8,128)(2,1)} %param.18) | copy-start | bytes 331780
  8.1 0.7 copy-start.5
  14.6 0.7 copy-start.3
  14.6 0.7 copy-start.4
  66.1 1.0 %copy-start = (bf16[1280,128]{1,0:T(8,128)(2,1)S(1)}, bf16[1280,128]{1,0:T(8,128)(2,1)}, u32[]{:S(2)}) copy-start(bf16[1280,128]{1,0:T(8,128)(2,1)} %get-tuple-element.10.refs_0_) | copy-start | bytes 983044
